TPU v7x, 512 devices: a whole 4x8x8 slice. The times are simulated.
512 devices in a mesh: row: 32 (over x, z), col: 16 (over y, core).
Axes of the slice: x: 4, y: 8, z: 8, core: 2. Of those that a mesh axis runs over, the one named last changes fastest.
Arguments:
- features: bfloat16 [1024, 512, 256], P('row', 'col'), may hold values from -6 to 6
- tower_weight: bfloat16 [2, 3, 3, 256, 256], replicated, may hold values from -0.1875 to 0.1875
- tower_bias: float32 [2, 256], replicated, may hold values from -3 to 3
- boxes: int32 [512, 4], P('row'), may hold values from 0 to 1023, as said below
- owner_slot: int32 [32, 16], P('row'), may hold values from 0 to 15, each once within a row
- mask_weight: bfloat16 [1, 3, 3, 256, 256], replicated, may hold values from -0.1875 to 0.1875
- mask_bias: float32 [1, 256], replicated, may hold values from -3 to 3
- deconv_weight: bfloat16 [2, 2, 256, 256], replicated, may hold values from -0.375 to 0.375
- deconv_bias: float32 [256], replicated, may hold values from -3 to 3
Outputs:
- tower: bfloat16 [1024, 512, 256], P('row', 'col')
- masks: bfloat16 [512, 28, 28, 256], P(('row', 'col'))
Inputs may be any that keep to these rules, and one draw needn't show every extreme that they name: `boxes`: row k is (top, left, height, width) of region k in feature pixels: the box lies inside the image, height 1 to 32, width 1 to 64, and its top row is among rows 32 * g to 32 * g + 31 with g = k // 16. The first region of every group has height 32 and width 64. Region 0 has top 0 and left 0; the last region is the single pixel at the image's bottom right corner.
All inputs are finite; a program needn't handle non-finite values.
Results may differ from a plain program's by a relative error of at most 0.0066.
Values may be sent and summed in bfloat16 or wider, within the bound.
No kernel may reach another device: no remote copies, remote signals or barrier semaphores. Data moves between devices by JAX's collectives and lax.ppermute only.
A program may use at most 64 MiB of HBM per device.

v0:
```python
import jax
import jax.numpy as jnp
from jax import lax
from jax.sharding import PartitionSpec as P

POOL = 14


def padded_2(value, sides, width):
    for axis, dim in sides:
        peers, length = (lax.axis_size(axis), value.shape[dim])
        up = [(i, (i + 1) % peers) for i in range(peers - 1)]
        down = [(j, i) for i, j in up]
        last = lax.slice_in_dim(value, length - width, length, axis=dim)
        leading = lax.slice_in_dim(value, 0, width, axis=dim)
        before = lax.ppermute(last, axis, up)
        after = lax.ppermute(leading, axis, down)
        value = jnp.concatenate([before, value, after], axis=dim)
    return value


def from_behind(block, axis, distance):
    devices = range(lax.axis_size(axis))
    route = [(i - distance, i) for i in devices if i - distance in devices]
    return lax.ppermute(block, axis, route)


def convolve(padded, kernel, bias_row):
    rows_out = padded.shape[-3] - 2
    cols_out = padded.shape[-2] - 2
    leading = padded.shape[:-3]
    channels = kernel.shape[-1]
    running = None
    for row_step in range(3):
        for col_step in range(3):
            window = padded[..., row_step : row_step + rows_out, col_step : col_step + cols_out, :]
            window = window.reshape(-1, padded.shape[-1])
            product = jnp.dot(
                window, kernel[row_step, col_step], preferred_element_type=jnp.float32
            )
            running = product if running is None else running + product
    running = jnp.maximum(running + bias_row, 0.0)
    return running.reshape(leading + (rows_out, cols_out, channels)).astype(jnp.bfloat16)


def bilinear_ramp(lower, extent, coords):
    lower_f = lower.astype(jnp.float32)[:, None, None]
    extent_f = extent.astype(jnp.float32)[:, None, None]
    bins = jnp.arange(POOL).astype(jnp.float32)[None, :, None]
    centre = lower_f + (bins + 0.5) * extent_f / POOL - 0.5
    centre = jnp.clip(centre, lower_f, lower_f + extent_f - 1.0)
    places = coords.astype(jnp.float32)[None, None, :]
    return jnp.maximum(1.0 - jnp.abs(places - centre), 0.0).astype(jnp.bfloat16)


def project(down_f, across, band_part):
    partial_sum = jnp.einsum("rqx,yxc->ryqc", across, band_part, preferred_element_type=jnp.float32)
    return jnp.einsum("rpy,ryqc->rpqc", down_f, partial_sum, precision=lax.Precision.HIGHEST)


def mask_head(pooled, mask_weight, mask_bias, deconv_weight, deconv_bias):
    hidden = pooled
    padded = jnp.pad(hidden, ((0, 0), (1, 1), (1, 1), (0, 0)))
    hidden = convolve(padded, mask_weight[0], mask_bias[0])
    lifted = jnp.einsum(
        "rabc,uvcd->raubvd", hidden, deconv_weight, preferred_element_type=jnp.float32
    )
    lifted = jnp.maximum(lifted + deconv_bias, 0.0)
    return lifted.reshape(hidden.shape[0], 2 * POOL, 2 * POOL, -1).astype(jnp.bfloat16)


def per_device(
    features,
    tower_weight,
    tower_bias,
    boxes,
    owner_slot,
    mask_weight,
    mask_bias,
    deconv_weight,
    deconv_bias,
):
    tile_rows, tile_cols, channels = features.shape
    current = features
    for layer_index in range(tower_weight.shape[0]):
        padded = padded_2(current, (("row", 0), ("col", 1)), 1)
        current = convolve(padded, tower_weight[layer_index], tower_bias[layer_index])
    below_tile = from_behind(current, "row", -1)
    band_tile = jnp.concatenate([current, below_tile], axis=0)
    band_first = lax.axis_index("row") * tile_rows
    band_coords = band_first + jnp.arange(2 * tile_rows, dtype=jnp.int32)
    group_size = boxes.shape[0]
    slot_of = owner_slot[0]
    picked = (slot_of[None, :] == jnp.arange(group_size, dtype=jnp.int32)[:, None]).astype(
        jnp.int32
    )
    ordered = jnp.sum(picked[:, :, None] * boxes[None, :, :], axis=1)
    per_owner = group_size // lax.axis_size("col")
    down_all = bilinear_ramp(ordered[:, 0], ordered[:, 2], band_coords).astype(jnp.float32)
    first_owned = lax.axis_index("col") * per_owner
    owned_boxes = lax.dynamic_slice_in_dim(ordered, first_owned, per_owner, 0)
    owned_down = lax.dynamic_slice_in_dim(down_all, first_owned, per_owner, 0)
    piece = lax.all_gather(band_tile, "col", axis=1, tiled=True)
    columns = jnp.arange(piece.shape[1], dtype=jnp.int32)
    across = bilinear_ramp(owned_boxes[:, 1], owned_boxes[:, 3], columns)
    pooled = project(owned_down, across, piece)
    masks = mask_head(
        pooled.astype(jnp.bfloat16), mask_weight, mask_bias, deconv_weight, deconv_bias
    )
    return (current, masks)


def solution(mesh):
    placed = (P("row", "col", None), P(), P(), P("row", None), P("row", None), P(), P(), P(), P())
    return jax.shard_map(
        per_device,
        mesh=mesh,
        in_specs=placed,
        out_specs=(P("row", "col", None), P(("row", "col"), None, None, None)),
        check_vma=False,
    )
```

profile of v0, /device:TPU:1, one launch (start us, length us, event | category | flops | bytes accessed | tf_op | source)
XLA Modules:
  0.0 197.2 jit_solution(13642533181125782840)
XLA Ops:
  7.2 0.8 fusion.49
  8.0 1.3 collective-permute-start.1
  9.3 5.6 %collective-permute-start = (bf16[1,32,256]{2,1,0:T(8,128)(2,1)S(1)}, bf16[1,32,256]{2,1,0:T(8,128)(2,1)S(1)}, u32[]{:S(2)}, u32[]{:S(2)}) collective-permute-start(bf16[1,32,256]{2,1,0:T(8,128)(2,1)S(1)} %get-tuple-element.33), channel_id=1, source_target_pairs={{0,16},{16,32},{32,48},{48,64},{64,80},{80,96},{96,112},{112,128},... | collective-permute-start | bytes 49160 | tf_op jit(solution)/shard_map/ppermute | solution.py:16
  14.9 1.8 slice_bitcast_fusion
  17.0 4.0 %collective-permute-start.2 = (bf16[34,1,256]{2,1,0:T(2,128)(2,1)S(1)}, bf16[34,1,256]{2,1,0:T(2,128)(2,1)S(1)}, u32[]{:S(2)}, u32[]{:S(2)}) collective-permute-start(bf16[34,1,256]{2,1,0:T(2,128)(2,1)S(1)} %get-tuple-element.23), channel_id=1, source_target_pairs={{0,1},{1,2},{2,3},{3,4},{4,5},{5,6},{6,7},{7,8},{8,9},{9,10},{10,1... | collective-permute-start | bytes 52232 | tf_op jit(solution)/shard_map/ppermute | solution.py:16
  21.1 5.1 %collective-permute-start.3 = (bf16[34,1,256]{2,1,0:T(2,128)(2,1)S(1)}, bf16[34,1,256]{2,1,0:T(2,128)(2,1)S(1)}, u32[]{:S(2)}, u32[]{:S(2)}) collective-permute-start(bf16[34,1,256]{2,1,0:T(2,128)(2,1)S(1)} %get-tuple-element.24), channel_id=1, source_target_pairs={{1,0},{2,1},{3,2},{4,3},{5,4},{6,5},{7,6},{8,7},{9,8},{10,9},{11,1... | collective-permute-start | bytes 52232 | tf_op jit(solution)/shard_map/ppermute | solution.py:17
  26.2 0.3 fusion.26
  26.5 0.3 fusion.27
  26.8 0.2 collective-permute-done.3
  27.1 0.9 pad_maximum_fusion.6
  27.9 0.3 fusion.25
  28.2 0.3 convolution_add_fusion.12
  28.5 0.3 convolution_add_fusion.11
  28.8 0.3 convolution_add_fusion.10
  29.1 0.3 convolution_add_fusion.9
  29.4 0.3 convolution_add_fusion.8
  29.7 0.4 fusion.8
  30.2 3.5 %collective-permute-start.4 = (bf16[1,32,256]{2,1,0:T(8,128)(2,1)S(1)}, bf16[1,32,256]{2,1,0:T(8,128)(2,1)S(1)}, u32[]{:S(2)}, u32[]{:S(2)}) collective-permute-start(bf16[1,32,256]{2,1,0:T(8,128)(2,1)S(1)} %get-tuple-element.27), channel_id=1, source_target_pairs={{0,16},{16,32},{32,48},{48,64},{64,80},{80,96},{96,112},{112,128},... | collective-permute-start | bytes 49160 | tf_op jit(solution)/shard_map/ppermute | solution.py:16
  33.7 1.3 collective-permute-start.5
  35.0 3.6 %collective-permute-done.5 = bf16[1,32,256]{2,1,0:T(8,128)(2,1)S(1)} collective-permute-done((bf16[1,32,256]{2,1,0:T(8,128)(2,1)S(1)}, bf16[1,32,256]{2,1,0:T(8,128)(2,1)S(1)}, u32[]{:S(2)}, u32[]{:S(2)}) %collective-permute-start.5) | collective-permute-done | bytes 16416 | tf_op jit(solution)/shard_map/ppermute | solution.py:17
  38.6 3.1 %collective-permute-start.6 = (bf16[34,1,256]{2,1,0:T(2,128)(2,1)S(1)}, bf16[34,1,256]{2,1,0:T(2,128)(2,1)S(1)}, u32[]{:S(2)}, u32[]{:S(2)}) collective-permute-start(bf16[34,1,256]{2,1,0:T(2,128)(2,1)S(1)} %get-tuple-element.18), channel_id=1, source_target_pairs={{0,1},{1,2},{2,3},{3,4},{4,5},{5,6},{6,7},{7,8},{8,9},{9,10},{10,1... | collective-permute-start | bytes 52232 | tf_op jit(solution)/shard_map/ppermute | solution.py:16
  41.7 1.9 collective-permute-start.7
  43.7 0.3 fusion.24
  44.0 2.9 %collective-permute-done.7 = bf16[34,1,256]{2,1,0:T(2,128)(2,1)S(1)} collective-permute-done((bf16[34,1,256]{2,1,0:T(2,128)(2,1)S(1)}, bf16[34,1,256]{2,1,0:T(2,128)(2,1)S(1)}, u32[]{:S(2)}, u32[]{:S(2)}) %collective-permute-start.7) | collective-permute-done | bytes 17440 | tf_op jit(solution)/shard_map/ppermute | solution.py:17
  47.0 0.4 maximum_maximum_fusion
  47.4 0.4 fusion.46
  47.8 0.3 convolution_add_fusion.6
  48.1 0.3 convolution_add_fusion.5
  48.4 0.3 convolution_add_fusion.4
  48.7 0.3 convolution_add_fusion.3
  49.0 0.3 fusion.23
  49.3 0.3 convolution_add_fusion.2
  49.6 0.3 convolution_add_fusion.1
  49.9 0.3 fusion.7
  50.3 1.6 collective-permute-start.8
  51.9 14.0 %collective-permute-done.8 = bf16[32,32,256]{2,1,0:T(8,128)(2,1)S(1)} collective-permute-done((bf16[32,32,256]{2,1,0:T(8,128)(2,1)S(1)}, bf16[32,32,256]{2,1,0:T(8,128)(2,1)S(1)}, u32[]{:S(2)}, u32[]{:S(2)}) %collective-permute-start.8) | collective-permute-done | bytes 524320 | tf_op jit(solution)/shard_map/ppermute | solution.py:25
  65.9 1.1 pad_maximum_fusion
  67.2 0.6 fusion.50
  69.3 107.0 %all-gather.2.cloned.1.call-done = bf16[64,512,256]{2,1,0:T(8,128)(2,1)} async-done(((bf16[64,32,256]{2,1,0:T(8,128)(2,1)}), bf16[64,512,256]{2,1,0:T(8,128)(2,1)}) %all-gather.2.cloned.1.call-update) | async-done | bytes 16777232 | tf_op jit(solution)/shard_map/all_gather | solution.py:103
  176.3 8.1 %convolution_bitcast_fusion = f32[64,14,256]{2,1,0:T(8,128)S(1)} fusion(bf16[64,512,256]{2,1,0:T(8,128)(2,1)} %all-gather.2.cloned.1.call-done, f32[14]{0:T(128)S(1)} %maximum_minimum_fusion.1, f32[512]{0:T(512)S(1)} %iota_convert_fusion), kind=kOutput, calls=%fused_computation | convolution fusion | flops 234916864 | bytes 17696824 | tf_op jit(solution)/shard_map/rqx,yxc->ryqc/dot_general | solution.py:57
  184.4 0.9 convolution_convert_fusion
  186.2 0.8 copy-done.3
  187.1 0.2 convolution_add_fusion.20
  187.4 0.2 convolution_add_fusion.19
  188.5 0.2 fusion.15
  188.8 0.3 fusion.12
  189.1 0.3 copy.35
  189.4 0.9 convert_element_type.147
  (69 shorter events, 2.7 us)
Async XLA Ops:
  7.2 181.6 %copy-start = (bf16[2,2,256,256]{3,2,1,0:T(8,128)(2,1)S(1)}, bf16[2,2,256,256]{3,2,1,0:T(8,128)(2,1)}, u32[]{:S(2)}) copy-start(bf16[2,2,256,256]{3,2,1,0:T(8,128)(2,1)} %param.16) | copy-start | bytes 1572868
  7.2 169.1 %all-gather.2.cloned.1.call-start = ((), (), s32[]{:S(2)}) async-start(), calls=%async_computation | async-start | bytes 17825792 | tf_op jit(solution)/shard_map/all_gather | solution.py:103
  8.0 8.8 %collective-permute-start.1 = (bf16[1,32,256]{2,1,0:T(8,128)(2,1)S(1)}, bf16[1,32,256]{2,1,0:T(8,128)(2,1)S(1)}, u32[]{:S(2)}, u32[]{:S(2)}) collective-permute-start(bf16[1,32,256]{2,1,0:T(8,128)(2,1)S(1)} %get-tuple-element.32), channel_id=1, source_target_pairs={{16,0},{32,16},{48,32},{64,48},{80,64},{96,80},{112,96},{128,112},... | collective-permute-start | bytes 49160 | tf_op jit(solution)/shard_map/ppermute | solution.py:17
  9.3 7.4 %copy-start.4 = (f32[2,256]{1,0:T(2,128)S(1)}, f32[2,256]{1,0:T(2,128)}, u32[]{:S(2)}) copy-start(f32[2,256]{1,0:T(2,128)} %param.11) | copy-start | bytes 6148
  9.3 7.5 %copy-start.1 = (bf16[32,32,256]{2,1,0:T(8,128)(2,1)S(1)}, bf16[32,32,256]{2,1,0:T(8,128)(2,1)}, u32[]{:S(2)}) copy-start(bf16[32,32,256]{2,1,0:T(8,128)(2,1)} %param.9) | copy-start | bytes 1572868
  9.3 7.4 %collective-permute-start = (bf16[1,32,256]{2,1,0:T(8,128)(2,1)S(1)}, bf16[1,32,256]{2,1,0:T(8,128)(2,1)S(1)}, u32[]{:S(2)}, u32[]{:S(2)}) collective-permute-start(bf16[1,32,256]{2,1,0:T(8,128)(2,1)S(1)} %get-tuple-element.33), channel_id=1, source_target_pairs={{0,16},{16,32},{32,48},{48,64},{64,80},{80,96},{96,112},{112,128},... | collective-permute-start | bytes 49160 | tf_op jit(solution)/shard_map/ppermute | solution.py:16
  17.0 9.8 %collective-permute-start.2 = (bf16[34,1,256]{2,1,0:T(2,128)(2,1)S(1)}, bf16[34,1,256]{2,1,0:T(2,128)(2,1)S(1)}, u32[]{:S(2)}, u32[]{:S(2)}) collective-permute-start(bf16[34,1,256]{2,1,0:T(2,128)(2,1)S(1)} %get-tuple-element.23), channel_id=1, source_target_pairs={{0,1},{1,2},{2,3},{3,4},{4,5},{5,6},{6,7},{7,8},{8,9},{9,10},{10,1... | collective-permute-start | bytes 52232 | tf_op jit(solution)/shard_map/ppermute | solution.py:16
  21.1 6.0 %collective-permute-start.3 = (bf16[34,1,256]{2,1,0:T(2,128)(2,1)S(1)}, bf16[34,1,256]{2,1,0:T(2,128)(2,1)S(1)}, u32[]{:S(2)}, u32[]{:S(2)}) collective-permute-start(bf16[34,1,256]{2,1,0:T(2,128)(2,1)S(1)} %get-tuple-element.24), channel_id=1, source_target_pairs={{1,0},{2,1},{3,2},{4,3},{5,4},{6,5},{7,6},{8,7},{9,8},{10,9},{11,1... | collective-permute-start | bytes 52232 | tf_op jit(solution)/shard_map/ppermute | solution.py:17
  30.2 4.8 %collective-permute-start.4 = (bf16[1,32,256]{2,1,0:T(8,128)(2,1)S(1)}, bf16[1,32,256]{2,1,0:T(8,128)(2,1)S(1)}, u32[]{:S(2)}, u32[]{:S(2)}) collective-permute-start(bf16[1,32,256]{2,1,0:T(8,128)(2,1)S(1)} %get-tuple-element.27), channel_id=1, source_target_pairs={{0,16},{16,32},{32,48},{48,64},{64,80},{80,96},{96,112},{112,128},... | collective-permute-start | bytes 49160 | tf_op jit(solution)/shard_map/ppermute | solution.py:16
  33.7 4.9 %collective-permute-start.5 = (bf16[1,32,256]{2,1,0:T(8,128)(2,1)S(1)}, bf16[1,32,256]{2,1,0:T(8,128)(2,1)S(1)}, u32[]{:S(2)}, u32[]{:S(2)}) collective-permute-start(bf16[1,32,256]{2,1,0:T(8,128)(2,1)S(1)} %get-tuple-element.28), channel_id=1, source_target_pairs={{16,0},{32,16},{48,32},{64,48},{80,64},{96,80},{112,96},{128,112},... | collective-permute-start | bytes 49160 | tf_op jit(solution)/shard_map/ppermute | solution.py:17
  38.6 5.4 %collective-permute-start.6 = (bf16[34,1,256]{2,1,0:T(2,128)(2,1)S(1)}, bf16[34,1,256]{2,1,0:T(2,128)(2,1)S(1)}, u32[]{:S(2)}, u32[]{:S(2)}) collective-permute-start(bf16[34,1,256]{2,1,0:T(2,128)(2,1)S(1)} %get-tuple-element.18), channel_id=1, source_target_pairs={{0,1},{1,2},{2,3},{3,4},{4,5},{5,6},{6,7},{7,8},{8,9},{9,10},{10,1... | collective-permute-start | bytes 52232 | tf_op jit(solution)/shard_map/ppermute | solution.py:16
  41.7 5.3 %collective-permute-start.7 = (bf16[34,1,256]{2,1,0:T(2,128)(2,1)S(1)}, bf16[34,1,256]{2,1,0:T(2,128)(2,1)S(1)}, u32[]{:S(2)}, u32[]{:S(2)}) collective-permute-start(bf16[34,1,256]{2,1,0:T(2,128)(2,1)S(1)} %get-tuple-element.19), channel_id=1, source_target_pairs={{1,0},{2,1},{3,2},{4,3},{5,4},{6,5},{7,6},{8,7},{9,8},{10,9},{11,1... | collective-permute-start | bytes 52232 | tf_op jit(solution)/shard_map/ppermute | solution.py:17
  50.2 16.7 %copy-start.2 = (bf16[1024,256]{1,0:T(8,128)(2,1)}, bf16[1024,256]{1,0:T(8,128)(2,1)S(1)}, u32[]{:S(2)}) copy-start(bf16[1024,256]{1,0:T(8,128)(2,1)S(1)} %fusion.7) | copy-start | bytes 1572868
  50.2 16.7 %copy-start.8 = (s32[1,16]{1,0:T(1,128)S(1)}, s32[1,16]{1,0:T(1,128)}, u32[]{:S(2)}) copy-start(s32[1,16]{1,0:T(1,128)} %param.13) | copy-start | bytes 196
  50.3 16.7 %copy-start.5 = (s32[16,4]{0,1:T(4,128)S(1)}, s32[16,4]{0,1:T(4,128)}, u32[]{:S(2)}) copy-start(s32[16,4]{0,1:T(4,128)} %param.12) | copy-start | bytes 772
  50.3 15.6 %collective-permute-start.8 = (bf16[32,32,256]{2,1,0:T(8,128)(2,1)S(1)}, bf16[32,32,256]{2,1,0:T(8,128)(2,1)S(1)}, u32[]{:S(2)}, u32[]{:S(2)}) collective-permute-start(bf16[32,32,256]{2,1,0:T(8,128)(2,1)S(1)} %bitcast.202), channel_id=1, source_target_pairs={{16,0},{32,16},{48,32},{64,48},{80,64},{96,80},{112,96},{128,112},... | collective-permute-start | bytes 1572872 | tf_op jit(solution)/shard_map/ppermute | solution.py:25
  185.7 1.3 copy-start.3
  187.7 0.8 copy-start.6
  188.1 0.7 copy-start.7
Sparse Core Ops, SparseCore 0:
  67.1 109.1 all-gather.1
where the time goes:
time: 198 us; the launch traced here: 197 us
  waiting for transfers between devices  128 us (65%)
  starting transfers between devices  27.5 us (14%)
  matrix products  16.4 us (8%)
  between operations  16 us (8%)
  local copies, waits for them, and re-layouts  6.62 us (3%)
  other arithmetic  2.9 us (1%)
    all_gather x1, waiting for transfers between devices, per_device(): piece = lax.all_gather(band_tile, 'col', axis=1, tiled=True)  107 us
    ppermute x4, starting transfers between devices, padded_2(): before = lax.ppermute(last, axis, up)  16.2 us
    ppermute x1, waiting for transfers between devices, from_behind(): return lax.ppermute(block, axis, route)  14 us
    ppermute x4, starting transfers between devices, padded_2(): after = lax.ppermute(leading, axis, down)  9.62 us
    dot_general x1, matrix products, project(): jnp.einsum('rqx,yxc->ryqc', across, band_part, preferred_element_type=jnp...  8.1 us
    dot_general x27, matrix products, convolve(): jnp.dot(window, kernel[row_step, col_step], preferred_element_type=jnp.fl...  7.13 us
    ppermute x4, waiting for transfers between devices, padded_2(): after = lax.ppermute(leading, axis, down)  6.75 us
  transfers between devices with their start and end apart: 10, of which 5 were waited for; matrix products, arithmetic and copies ran while one was open for 2% of the time, Pallas kernels for 0%

commit v1 on v0

--- a/solution.py
+++ b/solution.py
@@ -100,7 +100,9 @@
     first_owned = lax.axis_index("col") * per_owner
     owned_boxes = lax.dynamic_slice_in_dim(ordered, first_owned, per_owner, 0)
     owned_down = lax.dynamic_slice_in_dim(down_all, first_owned, per_owner, 0)
-    piece = lax.all_gather(band_tile, "col", axis=1, tiled=True)
+    piece = jnp.concatenate(
+        lax.all_to_all(jnp.stack([band_tile] * lax.axis_size("col")), "col", 0, 0), axis=1
+    )
     columns = jnp.arange(piece.shape[1], dtype=jnp.int32)
     across = bilinear_ramp(owned_boxes[:, 1], owned_boxes[:, 3], columns)
     pooled = project(owned_down, across, piece)

time: 198 us -> 460 us (2.32)
  waiting for transfers between devices: 128 us -> 387 us
  local copies, waits for them, and re-layouts: 6.62 us -> 20.8 us
  between operations: 16 us -> 2.6 us
  starting transfers between devices: 27.5 us -> 33.9 us
  matrix products: 16.4 us -> 10.7 us
    all_to_all x0 -> x1, waiting for transfers between devices: none -> 361 us  [per_device(): lax.all_to_all(jnp.stack([band_tile] * lax.axis_size('col')), 'col', 0, 0)]
    all_gather x1 -> x0, waiting for transfers between devices: 107 us -> none  [per_device(): piece = lax.all_gather(band_tile, 'col', axis=1, tiled=True)]
    all_to_all x0 -> x1, starting transfers between devices: none -> 9.01 us  [per_device(): lax.all_to_all(jnp.stack([band_tile] * lax.axis_size('col')), 'col', 0, 0)]
    reshape x0 -> x1, local copies, waits for them, and re-layouts: none -> 8.28 us  [per_device(): jnp.concatenate(lax.all_to_all(jnp.stack([band_tile] * lax.axis_size('col...]
    another operation x0 -> x1, local copies, waits for them, and re-layouts: none -> 6 us  [per_device(): jnp.stack([band_tile] * lax.axis_size('col'))]
    dot_general x1, matrix products: 8.1 us -> 2.33 us  [project(): jnp.einsum('rqx,yxc->ryqc', across, band_part, preferred_element_type=jnp...]
    ppermute x4, waiting for transfers between devices: 6.75 us -> 12.4 us  [padded_2(): after = lax.ppermute(leading, axis, down)]
  transfers between devices with their start and end apart: 10 -> 10, of which waited for: 5 -> 6; matrix products, arithmetic and copies ran while one was open for 2% -> 1% of each run, Pallas kernels for 0% -> 0%
where the time goes in v1:
time: 460 us; the launch traced here: 457 us
  waiting for transfers between devices  387 us (84%)
  starting transfers between devices  33.9 us (7%)
  local copies, waits for them, and re-layouts  20.8 us (5%)
  matrix products  10.7 us (2%)
    all_to_all x1, waiting for transfers between devices, per_device(): lax.all_to_all(jnp.stack([band_tile] * lax.axis_size('col')), 'col', 0, 0)  361 us
    ppermute x4, starting transfers between devices, padded_2(): before = lax.ppermute(last, axis, up)  16.8 us
    ppermute x1, waiting for transfers between devices, from_behind(): return lax.ppermute(block, axis, route)  13.8 us
    ppermute x4, waiting for transfers between devices, padded_2(): after = lax.ppermute(leading, axis, down)  12.4 us
  transfers between devices with their start and end apart: 10, of which 6 were waited for; matrix products, arithmetic and copies ran while one was open for 1% of the time, Pallas kernels for 0%

profile of v1, /device:TPU:1, one launch (start us, length us, event | category | flops | bytes accessed | tf_op | source)
XLA Modules:
  0.0 457.1 jit_solution(14243577590869140808)
XLA Ops:
  0.6 0.8 fusion.49
  1.4 4.8 %collective-permute-start = (bf16[1,32,256]{2,1,0:T(8,128)(2,1)S(1)}, bf16[1,32,256]{2,1,0:T(8,128)(2,1)S(1)}, u32[]{:S(2)}, u32[]{:S(2)}) collective-permute-start(bf16[1,32,256]{2,1,0:T(8,128)(2,1)S(1)} %get-tuple-element.33), channel_id=1, source_target_pairs={{0,16},{16,32},{32,48},{48,64},{64,80},{80,96},{96,112},{112,128},... | collective-permute-start | bytes 49160 | tf_op jit(solution)/shard_map/ppermute | solution.py:16
  6.3 1.4 collective-permute-start.1
  7.7 1.8 slice_bitcast_fusion
  9.6 2.0 collective-permute-done.1
  11.8 4.9 %collective-permute-start.2 = (bf16[34,1,256]{2,1,0:T(2,128)(2,1)S(1)}, bf16[34,1,256]{2,1,0:T(2,128)(2,1)S(1)}, u32[]{:S(2)}, u32[]{:S(2)}) collective-permute-start(bf16[34,1,256]{2,1,0:T(2,128)(2,1)S(1)} %get-tuple-element.23), channel_id=1, source_target_pairs={{0,1},{1,2},{2,3},{3,4},{4,5},{5,6},{6,7},{7,8},{8,9},{9,10},{10,1... | collective-permute-start | bytes 52232 | tf_op jit(solution)/shard_map/ppermute | solution.py:16
  16.7 2.1 collective-permute-start.3
  18.8 0.3 fusion.27
  19.1 0.3 fusion.26
  19.4 2.5 collective-permute-done.3
  22.0 0.9 pad_maximum_fusion.6
  22.8 0.3 fusion.25
  23.1 0.3 convolution_add_fusion.12
  23.4 0.3 convolution_add_fusion.11
  23.7 0.3 convolution_add_fusion.10
  24.0 0.3 convolution_add_fusion.9
  24.3 0.3 convolution_add_fusion.8
  24.6 0.4 fusion.8
  25.1 4.0 collective-permute-start.4
  29.1 1.3 collective-permute-start.5
  30.4 5.0 %collective-permute-done.5 = bf16[1,32,256]{2,1,0:T(8,128)(2,1)S(1)} collective-permute-done((bf16[1,32,256]{2,1,0:T(8,128)(2,1)S(1)}, bf16[1,32,256]{2,1,0:T(8,128)(2,1)S(1)}, u32[]{:S(2)}, u32[]{:S(2)}) %collective-permute-start.5) | collective-permute-done | bytes 16416 | tf_op jit(solution)/shard_map/ppermute | solution.py:17
  35.5 3.1 collective-permute-start.6
  38.5 1.9 collective-permute-start.7
  40.5 0.3 fusion.24
  40.9 2.9 collective-permute-done.7
  43.8 0.4 maximum_maximum_fusion
  44.2 0.4 fusion.46
  44.7 0.3 convolution_add_fusion.6
  45.0 0.3 convolution_add_fusion.5
  45.3 0.3 convolution_add_fusion.4
  45.6 0.3 convolution_add_fusion.3
  45.9 0.3 fusion.23
  46.1 0.3 convolution_add_fusion.2
  46.5 0.3 convolution_add_fusion.1
  46.8 0.3 fusion.7
  47.1 1.3 collective-permute-start.8
  48.4 13.8 %collective-permute-done.8 = bf16[32,32,256]{2,1,0:T(8,128)(2,1)S(1)} collective-permute-done((bf16[32,32,256]{2,1,0:T(8,128)(2,1)S(1)}, bf16[32,32,256]{2,1,0:T(8,128)(2,1)S(1)}, u32[]{:S(2)}, u32[]{:S(2)}) %collective-permute-start.8) | collective-permute-done | bytes 524320 | tf_op jit(solution)/shard_map/ppermute | solution.py:25
  62.3 6.0 %stack.2 = bf16[16,64,32,256]{3,2,1,0:T(8,128)(2,1)} broadcast(bf16[64,32,256]{2,1,0:T(8,128)(2,1)S(1)} %pad_maximum_fusion), dimensions={1,2,3} | broadcast | bytes 17825792 | tf_op jit(solution)/shard_map/stack | solution.py:104
  68.3 9.0 %all-to-all-start = ((bf16[16,64,32,256]{3,2,1,0:T(8,128)(2,1)}), bf16[16,64,32,256]{3,2,1,0:T(8,128)(2,1)}, u32[]{:S(2)}, u32[]{:S(2)}) async-start(bf16[16,64,32,256]{3,2,1,0:T(8,128)(2,1)} %stack.2), calls=%async_computation | async-start | bytes 33554432 | tf_op jit(solution)/shard_map/all_to_all | solution.py:104
  77.5 0.5 fusion.50
  79.5 361.0 %all-to-all-done = bf16[16,64,32,256]{3,2,1,0:T(8,128)(2,1)} async-done(((bf16[16,64,32,256]{3,2,1,0:T(8,128)(2,1)}), bf16[16,64,32,256]{3,2,1,0:T(8,128)(2,1)}, u32[]{:S(2)}, u32[]{:S(2)}) %all-to-all-start) | async-done | bytes 16777248 | tf_op jit(solution)/shard_map/all_to_all | solution.py:104
  440.5 8.3 %copy.38 = bf16[64,16,32,256]{3,2,1,0:T(8,128)(2,1)S(1)} copy(bf16[64,16,32,256]{3,2,0,1:T(8,128)(2,1)} %bitcast.48) | data formatting | bytes 33554432 | tf_op jit(solution)/shard_map/reshape | solution.py:103
  448.8 2.3 convolution_bitcast_fusion
  451.1 0.9 convolution_convert_fusion
  453.0 0.8 copy-done.3
  455.6 0.3 fusion.12
  455.9 0.3 copy.49
  456.2 0.9 convert_element_type.148
  (70 shorter events, 3.3 us)
Async XLA Ops:
  0.6 454.9 %copy-start = (bf16[2,2,256,256]{3,2,1,0:T(8,128)(2,1)S(1)}, bf16[2,2,256,256]{3,2,1,0:T(8,128)(2,1)}, u32[]{:S(2)}) copy-start(bf16[2,2,256,256]{3,2,1,0:T(8,128)(2,1)} %param.16) | copy-start | bytes 1572868
  1.4 8.1 %collective-permute-start = (bf16[1,32,256]{2,1,0:T(8,128)(2,1)S(1)}, bf16[1,32,256]{2,1,0:T(8,128)(2,1)S(1)}, u32[]{:S(2)}, u32[]{:S(2)}) collective-permute-start(bf16[1,32,256]{2,1,0:T(8,128)(2,1)S(1)} %get-tuple-element.33), channel_id=1, source_target_pairs={{0,16},{16,32},{32,48},{48,64},{64,80},{80,96},{96,112},{112,128},... | collective-permute-start | bytes 49160 | tf_op jit(solution)/shard_map/ppermute | solution.py:16
  6.3 3.3 copy-start.4
  6.3 5.3 %copy-start.1 = (bf16[32,32,256]{2,1,0:T(8,128)(2,1)S(1)}, bf16[32,32,256]{2,1,0:T(8,128)(2,1)}, u32[]{:S(2)}) copy-start(bf16[32,32,256]{2,1,0:T(8,128)(2,1)} %param.9) | copy-start | bytes 1572868
  6.3 5.3 %collective-permute-start.1 = (bf16[1,32,256]{2,1,0:T(8,128)(2,1)S(1)}, bf16[1,32,256]{2,1,0:T(8,128)(2,1)S(1)}, u32[]{:S(2)}, u32[]{:S(2)}) collective-permute-start(bf16[1,32,256]{2,1,0:T(8,128)(2,1)S(1)} %get-tuple-element.32), channel_id=1, source_target_pairs={{16,0},{32,16},{48,32},{64,48},{80,64},{96,80},{112,96},{128,112},... | collective-permute-start | bytes 49160 | tf_op jit(solution)/shard_map/ppermute | solution.py:17
  11.8 7.7 %collective-permute-start.2 = (bf16[34,1,256]{2,1,0:T(2,128)(2,1)S(1)}, bf16[34,1,256]{2,1,0:T(2,128)(2,1)S(1)}, u32[]{:S(2)}, u32[]{:S(2)}) collective-permute-start(bf16[34,1,256]{2,1,0:T(2,128)(2,1)S(1)} %get-tuple-element.23), channel_id=1, source_target_pairs={{0,1},{1,2},{2,3},{3,4},{4,5},{5,6},{6,7},{7,8},{8,9},{9,10},{10,1... | collective-permute-start | bytes 52232 | tf_op jit(solution)/shard_map/ppermute | solution.py:16
  16.7 5.3 %collective-permute-start.3 = (bf16[34,1,256]{2,1,0:T(2,128)(2,1)S(1)}, bf16[34,1,256]{2,1,0:T(2,128)(2,1)S(1)}, u32[]{:S(2)}, u32[]{:S(2)}) collective-permute-start(bf16[34,1,256]{2,1,0:T(2,128)(2,1)S(1)} %get-tuple-element.24), channel_id=1, source_target_pairs={{1,0},{2,1},{3,2},{4,3},{5,4},{6,5},{7,6},{8,7},{9,8},{10,9},{11,1... | collective-permute-start | bytes 52232 | tf_op jit(solution)/shard_map/ppermute | solution.py:17
  25.1 5.3 %collective-permute-start.4 = (bf16[1,32,256]{2,1,0:T(8,128)(2,1)S(1)}, bf16[1,32,256]{2,1,0:T(8,128)(2,1)S(1)}, u32[]{:S(2)}, u32[]{:S(2)}) collective-permute-start(bf16[1,32,256]{2,1,0:T(8,128)(2,1)S(1)} %get-tuple-element.27), channel_id=1, source_target_pairs={{0,16},{16,32},{32,48},{48,64},{64,80},{80,96},{96,112},{112,128},... | collective-permute-start | bytes 49160 | tf_op jit(solution)/shard_map/ppermute | solution.py:16
  29.1 6.3 %collective-permute-start.5 = (bf16[1,32,256]{2,1,0:T(8,128)(2,1)S(1)}, bf16[1,32,256]{2,1,0:T(8,128)(2,1)S(1)}, u32[]{:S(2)}, u32[]{:S(2)}) collective-permute-start(bf16[1,32,256]{2,1,0:T(8,128)(2,1)S(1)} %get-tuple-element.28), channel_id=1, source_target_pairs={{16,0},{32,16},{48,32},{64,48},{80,64},{96,80},{112,96},{128,112},... | collective-permute-start | bytes 49160 | tf_op jit(solution)/shard_map/ppermute | solution.py:17
  35.5 5.4 %collective-permute-start.6 = (bf16[34,1,256]{2,1,0:T(2,128)(2,1)S(1)}, bf16[34,1,256]{2,1,0:T(2,128)(2,1)S(1)}, u32[]{:S(2)}, u32[]{:S(2)}) collective-permute-start(bf16[34,1,256]{2,1,0:T(2,128)(2,1)S(1)} %get-tuple-element.18), channel_id=1, source_target_pairs={{0,1},{1,2},{2,3},{3,4},{4,5},{5,6},{6,7},{7,8},{8,9},{9,10},{10,1... | collective-permute-start | bytes 52232 | tf_op jit(solution)/shard_map/ppermute | solution.py:16
  38.5 5.3 %collective-permute-start.7 = (bf16[34,1,256]{2,1,0:T(2,128)(2,1)S(1)}, bf16[34,1,256]{2,1,0:T(2,128)(2,1)S(1)}, u32[]{:S(2)}, u32[]{:S(2)}) collective-permute-start(bf16[34,1,256]{2,1,0:T(2,128)(2,1)S(1)} %get-tuple-element.19), channel_id=1, source_target_pairs={{1,0},{2,1},{3,2},{4,3},{5,4},{6,5},{7,6},{8,7},{9,8},{10,9},{11,1... | collective-permute-start | bytes 52232 | tf_op jit(solution)/shard_map/ppermute | solution.py:17
  47.1 21.2 %copy-start.2 = (bf16[1024,256]{1,0:T(8,128)(2,1)}, bf16[1024,256]{1,0:T(8,128)(2,1)S(1)}, u32[]{:S(2)}) copy-start(bf16[1024,256]{1,0:T(8,128)(2,1)S(1)} %fusion.7) | copy-start | bytes 1572868
  47.1 15.1 %collective-permute-start.8 = (bf16[32,32,256]{2,1,0:T(8,128)(2,1)S(1)}, bf16[32,32,256]{2,1,0:T(8,128)(2,1)S(1)}, u32[]{:S(2)}, u32[]{:S(2)}) collective-permute-start(bf16[32,32,256]{2,1,0:T(8,128)(2,1)S(1)} %bitcast.205), channel_id=1, source_target_pairs={{16,0},{32,16},{48,32},{64,48},{80,64},{96,80},{112,96},{128,112},... | collective-permute-start | bytes 1572872 | tf_op jit(solution)/shard_map/ppermute | solution.py:25
  68.3 9.0 %copy-start.8 = (s32[1,16]{1,0:T(1,128)S(1)}, s32[1,16]{1,0:T(1,128)}, u32[]{:S(2)}) copy-start(s32[1,16]{1,0:T(1,128)} %param.13) | copy-start | bytes 196
  68.3 9.0 %copy-start.5 = (s32[16,4]{0,1:T(4,128)S(1)}, s32[16,4]{0,1:T(4,128)}, u32[]{:S(2)}) copy-start(s32[16,4]{0,1:T(4,128)} %param.12) | copy-start | bytes 772
  68.3 372.3 %all-to-all-start = ((bf16[16,64,32,256]{3,2,1,0:T(8,128)(2,1)}), bf16[16,64,32,256]{3,2,1,0:T(8,128)(2,1)}, u32[]{:S(2)}, u32[]{:S(2)}) async-start(bf16[16,64,32,256]{3,2,1,0:T(8,128)(2,1)} %stack.2), calls=%async_computation | async-start | bytes 33554432 | tf_op jit(solution)/shard_map/all_to_all | solution.py:104
  452.5 1.3 copy-start.3
  454.5 0.8 copy-start.6
  454.9 0.7 copy-start.7
